TPU v7x, 32 devices: a whole 2x2x4 slice. The times are simulated.
32 devices in a mesh: leaf: 8 (over z, x), row: 4 (over y, core).
Axes of the slice: x: 2, y: 2, z: 4, core: 2. Of those that a mesh axis runs over, the one named last changes fastest.
Arguments:
- leaf_probes: bfloat16 [8, 2048, 128], P('leaf', 'row'), may hold values from -6 to 6
- lower_probes: bfloat16 [4, 4096, 128], P(None, ('leaf', 'row')), may hold values from -6 to 6
- middle_probes: bfloat16 [2, 8192, 128], P(None, ('leaf', 'row')), may hold values from -6 to 6
- root_probes: bfloat16 [16384, 128], P(('leaf', 'row')), may hold values from -6 to 6
- leaf_inverse: bfloat16 [8, 2048, 2048], P('leaf', 'row'), as said below
- lower_inverse: bfloat16 [4, 4096, 4096], P(None, 'row', 'leaf'), as said below
- middle_inverse: bfloat16 [2, 8192, 8192], P(None, 'row', 'leaf'), as said below
- root_inverse: bfloat16 [16384, 16384], P('row', 'leaf'), as said below
- leaf_panel: bfloat16 [8, 512, 2048], P('leaf', 'row'), may hold values from -0.09375 to 0.09375
- lower_to_middle: bfloat16 [4, 8192, 4096], P(None, 'leaf', 'row'), may hold values from -0.09375 to 0.09375
- lower_to_root: bfloat16 [4, 16384, 4096], P(None, 'leaf', 'row'), may hold values from -0.09375 to 0.09375
- middle_to_root: bfloat16 [2, 16384, 8192], P(None, 'leaf', 'row'), may hold values from -0.0625 to 0.0625
- leaf_parent: int32 [8], replicated, may hold values from 0 to 3
- leaf_blocks: int32 [8, 4], replicated, may hold values from 0 to 127, as said below
Outputs:
- leaf_solution: bfloat16 [8, 2048, 128], P('leaf', 'row')
- lower_solution: bfloat16 [4, 4096, 128], P(None, ('leaf', 'row'))
- middle_solution: bfloat16 [2, 8192, 128], P(None, ('leaf', 'row'))
- root_solution: bfloat16 [16384, 128], P(('leaf', 'row'))
Inputs may be any that keep to these rules, and one draw needn't show every extreme that they name: `leaf_inverse`: every inverse of a diagonal factor block is lower triangular: entries above its diagonal are zero. `lower_inverse`: every inverse of a diagonal factor block is lower triangular: entries above its diagonal are zero. `middle_inverse`: every inverse of a diagonal factor block is lower triangular: entries above its diagonal are zero. `root_inverse`: every inverse of a diagonal factor block is lower triangular: entries above its diagonal are zero. `leaf_blocks`: columns 0 and 1 are two different blocks of 128 rows of the parent separator, column 2 a block of the second-level separator above it, column 3 a block of the root.
All inputs are finite; a program needn't handle non-finite values.
Results may differ from a plain program's by a relative error of at most 0.04.
Values may be sent and summed in bfloat16 or wider, within the bound.
A program may use at most 128 MiB of HBM per device.

v0:
```python
import jax
import jax.numpy as jnp
from jax import lax
from jax.sharding import PartitionSpec as P

LOWER_ORDER = 4096
MIDDLE_ORDER = 8192
ROOT_ORDER = 16384
BLOCK = 128
PANEL = 512


def row_gather(pieces):
    return lax.all_gather(pieces, "row", axis=1, tiled=True)


def row_total(summands):
    return lax.psum_scatter(
        summands.astype(jnp.bfloat16), "row", scatter_dimension=1, tiled=True
    ).astype(jnp.float32)


def leaf_gather(pieces):
    return lax.all_gather(pieces, "leaf", axis=1, tiled=True)


def leaf_total(summands):
    return lax.psum_scatter(
        summands.astype(jnp.bfloat16), "leaf", scatter_dimension=1, tiled=True
    ).astype(jnp.float32)


def panel_targets(leaf_parent, leaf_blocks, length):
    row_ids = jnp.arange(length, dtype=jnp.int32)
    block_index = (row_ids // BLOCK)[None, :]
    offset = (row_ids % BLOCK)[None, :]
    chosen = jnp.where(
        block_index == 0,
        leaf_blocks[:, 0:1],
        jnp.where(
            block_index == 1,
            leaf_blocks[:, 1:2],
            jnp.where(block_index == 2, leaf_blocks[:, 2:3], leaf_blocks[:, 3:4]),
        ),
    )
    parent = leaf_parent[:, None]
    levels = jnp.where(block_index < 2, 2, jnp.where(block_index == 2, 1, 0)) + 0 * parent
    owners = jnp.where(block_index < 2, parent, jnp.where(block_index == 2, parent // 2, 0))
    return (levels, owners, chosen * BLOCK + offset)


def selector(targets, level_code, separators, window_start, window):
    levels, owners, places = targets
    inside = (levels == level_code) & (places >= window_start) & (places < window_start + window)
    flat_slot = jnp.where(inside, owners * window + places - window_start, -1).reshape(-1)
    slot_ids = jnp.arange(separators * window, dtype=jnp.int32)
    return (slot_ids[:, None] == flat_slot[None, :]).astype(jnp.bfloat16)


def level_forward(inverse, columns):
    summed_part = jnp.einsum("smn,snp->smp", inverse, columns, preferred_element_type=jnp.float32)
    return leaf_total(summed_part).astype(jnp.bfloat16)


def level_backward(inverse, row_block):
    summed_part = jnp.einsum("smn,smp->snp", inverse, row_block, preferred_element_type=jnp.float32)
    return row_total(summed_part).astype(jnp.bfloat16)


def body(
    leaf_probes,
    lower_probes,
    middle_probes,
    root_probes,
    leaf_inverse,
    lower_inverse,
    middle_inverse,
    root_inverse,
    leaf_panel,
    lower_to_middle,
    lower_to_root,
    middle_to_root,
    leaf_parent,
    leaf_blocks,
):
    leaf_devices = lax.axis_size("leaf")
    row_devices = lax.axis_size("row")
    leaf_index = lax.axis_index("leaf")
    row_index = lax.axis_index("row")
    position = leaf_index * row_devices + row_index
    probe_count = leaf_probes.shape[-1]
    root_pieces = root_probes[None]
    root_tiles = root_inverse[None]
    orders = (LOWER_ORDER, MIDDLE_ORDER, ROOT_ORDER)
    counts = (4, 2, 1)
    level_codes = (2, 1, 0)
    leaf_columns = row_gather(leaf_probes)
    leaf_solved = jnp.einsum(
        "lab,lbp->lap", leaf_inverse, leaf_columns, preferred_element_type=jnp.float32
    ).astype(jnp.bfloat16)
    leaf_whole = row_gather(leaf_solved)
    leaf_update = jnp.einsum(
        "lkb,lbp->lkp", leaf_panel, leaf_whole, preferred_element_type=jnp.float32
    ).astype(jnp.bfloat16)
    received = leaf_gather(row_gather(leaf_update))[0]
    targets = panel_targets(leaf_parent, leaf_blocks, PANEL)
    windows = [level_order // (leaf_devices * row_devices) for level_order in orders]
    pickers = [
        selector(
            targets,
            level_codes[member],
            counts[member],
            position * windows[member],
            windows[member],
        )
        for member in range(3)
    ]
    added = [
        jnp.dot(pickers[member], received, preferred_element_type=jnp.float32).reshape(
            counts[member], windows[member], probe_count
        )
        for member in range(3)
    ]
    lower_input = (lower_probes.astype(jnp.float32) - added[0]).astype(jnp.bfloat16)
    lower_solved = level_forward(lower_inverse, row_gather(lower_input))
    lower_block = leaf_gather(lower_solved)
    to_middle = jnp.einsum(
        "san,snp->sap", lower_to_middle, lower_block, preferred_element_type=jnp.float32
    )
    to_middle = to_middle.reshape(2, 2, to_middle.shape[1], probe_count).sum(axis=1)
    to_root = jnp.einsum(
        "san,snp->sap", lower_to_root, lower_block, preferred_element_type=jnp.float32
    ).sum(axis=0, keepdims=True)
    middle_total = row_total(to_middle) + added[1]
    middle_input = (middle_probes.astype(jnp.float32) - middle_total).astype(jnp.bfloat16)
    root_early = row_total(to_root)
    middle_solved = level_forward(middle_inverse, row_gather(middle_input))
    middle_block = leaf_gather(middle_solved)
    from_middle = jnp.einsum(
        "san,snp->sap", middle_to_root, middle_block, preferred_element_type=jnp.float32
    ).sum(axis=0, keepdims=True)
    root_total = root_early + row_total(from_middle)
    root_total = root_total + added[2]
    root_input = (root_pieces.astype(jnp.float32) - root_total).astype(jnp.bfloat16)
    root_solved = level_forward(root_tiles, row_gather(root_input))
    root_solution = level_backward(root_tiles, leaf_gather(root_solved))
    root_columns = row_gather(root_solution)
    middle_drop = jnp.einsum(
        "san,ap->snp", middle_to_root, root_columns[0], preferred_element_type=jnp.float32
    )
    middle_reduced = (middle_solved.astype(jnp.float32) - leaf_total(middle_drop)).astype(
        jnp.bfloat16
    )
    middle_solution = level_backward(middle_inverse, leaf_gather(middle_reduced))
    middle_columns = row_gather(middle_solution)
    parent_columns = jnp.repeat(middle_columns, 2, axis=0)
    lower_drop = jnp.einsum(
        "san,sap->snp", lower_to_middle, parent_columns, preferred_element_type=jnp.float32
    )
    lower_drop = lower_drop + jnp.einsum(
        "san,ap->snp", lower_to_root, root_columns[0], preferred_element_type=jnp.float32
    )
    lower_reduced = (lower_solved.astype(jnp.float32) - leaf_total(lower_drop)).astype(jnp.bfloat16)
    lower_solution = level_backward(lower_inverse, leaf_gather(lower_reduced))
    sources = (lower_solution, middle_solution, root_solution)
    values = sum(
        [
            jnp.einsum(
                "sm,sp->mp",
                pickers[member],
                sources[member].reshape(-1, probe_count),
                preferred_element_type=jnp.float32,
            )
            for member in range(3)
        ]
    )
    ancestor = row_total(leaf_total(values[None]))
    ancestor = ancestor.astype(jnp.bfloat16)
    leaf_back = row_total(
        jnp.einsum("lkb,lkp->lbp", leaf_panel, ancestor, preferred_element_type=jnp.float32)
    )
    leaf_reduced = (leaf_solved.astype(jnp.float32) - leaf_back).astype(jnp.bfloat16)
    leaf_solution = row_total(
        jnp.einsum("lab,lap->lbp", leaf_inverse, leaf_reduced, preferred_element_type=jnp.float32)
    ).astype(jnp.bfloat16)
    return (leaf_solution, lower_solution, middle_solution, root_solution[0])


def solution(mesh):
    placed = (
        P("leaf", "row", None),
        P(None, ("leaf", "row"), None),
        P(None, ("leaf", "row"), None),
        P(("leaf", "row"), None),
        P("leaf", "row", None),
        P(None, "row", "leaf"),
        P(None, "row", "leaf"),
        P("row", "leaf"),
        P("leaf", "row", None),
        P(None, "leaf", "row"),
        P(None, "leaf", "row"),
        P(None, "leaf", "row"),
        P(),
        P(),
    )
    return jax.shard_map(
        body,
        mesh=mesh,
        in_specs=placed,
        out_specs=(
            P("leaf", "row", None),
            P(None, ("leaf", "row"), None),
            P(None, ("leaf", "row"), None),
            P(("leaf", "row"), None),
        ),
        check_vma=False,
    )
```

profile of v0, /device:TPU:0, one launch (start us, length us, event | category | flops | bytes accessed | tf_op | source)
XLA Modules:
  0.0 1001.0 jit_solution(16060059342497954576)
XLA Ops:
  7.2 9.0 all_gather.42
  16.9 7.3 all-gather
  24.2 1.4 fusion.61
  25.6 5.9 all-gather.1
  32.3 0.8 slice_bitcast_fusion.3
  33.9 38.2 %all-gather.20.cloned.1.call-done = bf16[4096,128]{0,1:T(8,128)(2,1)} async-done(((bf16[512,128]{0,1:T(8,128)(2,1)}), bf16[4096,128]{0,1:T(8,128)(2,1)}) %all-gather.20.cloned.1.call-update) | async-done | bytes 1048592 | tf_op jit(solution)/shard_map/all_gather | solution.py:24
  72.1 2.6 fusion.57
  74.6 7.2 all_gather.46
  81.9 4.7 fusion.36
  86.5 1.7 copy.75
  88.3 1.1 copy.92
  89.5 61.8 %reduce-scatter.46.cloned.1.call-done = bf16[128,512]{1,0:T(8,128)(2,1)} async-done(((bf16[1024,512]{1,0:T(8,128)(2,1)}), bf16[128,512]{1,0:T(8,128)(2,1)}) %reduce-scatter.46.cloned.1.call-update) | async-done | bytes 131088
  151.3 0.9 reshape.491
  152.2 0.8 copy.76
  153.1 39.6 %all-gather.10.cloned.1.call-done = bf16[4,1024,128]{1,2,0:T(8,128)(2,1)} async-done(((bf16[4,128,128]{1,2,0:T(8,128)(2,1)}), bf16[4,1024,128]{1,2,0:T(8,128)(2,1)}) %all-gather.10.cloned.1.call-update) | async-done | bytes 1048592 | tf_op jit(solution)/shard_map/all_gather | solution.py:24
  192.7 6.7 bitcast_reduce_fusion
  199.4 1.0 copy.55
  200.6 20.5 %reduce-scatter.22.cloned.1.call-done = bf16[2,256,128]{2,1,0:T(8,128)(2,1)} async-done(((bf16[2,1024,128]{2,1,0:T(8,128)(2,1)}), bf16[2,256,128]{2,1,0:T(8,128)(2,1)}) %reduce-scatter.22.cloned.1.call-update) | async-done | bytes 131088 | tf_op jit(solution)/shard_map/reduce_scatter | solution.py:18
  221.1 2.8 fusion.51
  223.8 6.8 all_gather.48
  230.6 7.3 fusion.23
  238.0 64.3 %reduce-scatter.24.cloned.1.call-done = bf16[2,256,128]{1,2,0:T(8,128)(2,1)} async-done(((bf16[2,2048,128]{1,2,0:T(8,128)(2,1)}), bf16[2,256,128]{1,2,0:T(8,128)(2,1)}) %reduce-scatter.24.cloned.1.call-update) | async-done | bytes 131088 | tf_op jit(solution)/shard_map/reduce_scatter | solution.py:28
  302.6 12.2 %fusion.29 = bf16[1,2048,128]{1,2,0:T(8,128)(2,1)} fusion(bf16[4,1024,128]{1,2,0:T(8,128)(2,1)S(1)} %copy-done.1, bf16[4,2048,1024]{2,1,0:T(8,128)(2,1)} %param.24), kind=kOutput, calls=%fused_computation.39 | convolution fusion | flops 2147745792 | bytes 18350080 | tf_op jit(solution)/shard_map/san,snp->sap/dot_general | solution.py:131
  314.9 28.2 %all-gather.12.cloned.1.call-done = bf16[2,2048,128]{1,2,0:T(8,128)(2,1)} async-done(((bf16[2,256,128]{1,2,0:T(8,128)(2,1)}), bf16[2,2048,128]{1,2,0:T(8,128)(2,1)}) %all-gather.12.cloned.1.call-update) | async-done | bytes 1048592 | tf_op jit(solution)/shard_map/all_gather | solution.py:24
  343.0 12.5 %fusion.28 = bf16[1,2048,128]{1,2,0:T(8,128)(2,1)} fusion(bf16[2,2048,128]{1,2,0:T(8,128)(2,1)} %all-gather.12.cloned.1.call-done, bf16[2,2048,2048]{2,1,0:T(8,128)(2,1)} %param.25), kind=kOutput, calls=%fused_computation.38 | convolution fusion | flops 2147745792 | bytes 18350080 | tf_op jit(solution)/shard_map/san,snp->sap/dot_general | solution.py:139
  355.8 10.4 %reduce-scatter.26.cloned.1.call-done = bf16[1,512,128]{1,2,0:T(8,128)(2,1)} async-done(((bf16[1,2048,128]{1,2,0:T(8,128)(2,1)}), bf16[1,512,128]{1,2,0:T(8,128)(2,1)}) %reduce-scatter.26.cloned.1.call-update) | async-done | bytes 131088 | tf_op jit(solution)/shard_map/reduce_scatter | solution.py:18
  366.2 24.2 %reduce-scatter.28.cloned.1.call-done = bf16[1,512,128]{1,2,0:T(8,128)(2,1)} async-done(((bf16[1,2048,128]{1,2,0:T(8,128)(2,1)}), bf16[1,512,128]{1,2,0:T(8,128)(2,1)}) %reduce-scatter.28.cloned.1.call-update) | async-done | bytes 131088 | tf_op jit(solution)/shard_map/reduce_scatter | solution.py:18
  390.4 3.1 fusion.60
  393.5 7.0 all_gather.50
  400.5 12.4 %fusion.12 = bf16[1,4096,128]{1,2,0:T(8,128)(2,1)} fusion(bf16[4096,2048]{1,0:T(8,128)(2,1)} %param.21, bf16[1,2048,128]{1,2,0:T(8,128)(2,1)S(1)} %all_gather.50), kind=kOutput, calls=%fused_computation.16 | convolution fusion | flops 2148007936 | bytes 18350080 | tf_op jit(solution)/shard_map/smn,snp->smp/dot_general | solution.py:61
  412.9 64.5 %reduce-scatter.30.cloned.1.call-done = bf16[1,512,128]{1,2,0:T(8,128)(2,1)} async-done(((bf16[1,4096,128]{1,2,0:T(8,128)(2,1)}), bf16[1,512,128]{1,2,0:T(8,128)(2,1)}) %reduce-scatter.30.cloned.1.call-update) | async-done | bytes 131088 | tf_op jit(solution)/shard_map/reduce_scatter | solution.py:28
  477.5 40.4 %all-gather.14.cloned.1.call-done = bf16[1,4096,128]{1,2,0:T(8,128)(2,1)} async-done(((bf16[1,512,128]{1,2,0:T(8,128)(2,1)}), bf16[1,4096,128]{1,2,0:T(8,128)(2,1)}) %all-gather.14.cloned.1.call-update) | async-done | bytes 1048592 | tf_op jit(solution)/shard_map/all_gather | solution.py:24
  518.0 9.2 fusion.27
  527.3 20.7 %reduce-scatter.32.cloned.1.call-done = bf16[1,512,128]{1,2,0:T(8,128)(2,1)} async-done(((bf16[1,2048,128]{1,2,0:T(8,128)(2,1)}), bf16[1,512,128]{1,2,0:T(8,128)(2,1)}) %reduce-scatter.32.cloned.1.call-update) | async-done | bytes 131088 | tf_op jit(solution)/shard_map/reduce_scatter | solution.py:18
  547.9 7.0 all_gather.52
  554.9 9.1 fusion.24
  564.1 64.4 %reduce-scatter.34.cloned.1.call-done = bf16[2,256,128]{1,2,0:T(8,128)(2,1)} async-done(((bf16[2,2048,128]{1,2,0:T(8,128)(2,1)}), bf16[2,256,128]{1,2,0:T(8,128)(2,1)}) %reduce-scatter.34.cloned.1.call-update) | async-done | bytes 131088 | tf_op jit(solution)/shard_map/reduce_scatter | solution.py:28
  628.5 1.6 subtract_convert_fusion.1
  630.2 39.5 %all-gather.16.cloned.1.call-done = bf16[2,2048,128]{1,2,0:T(8,128)(2,1)} async-done(((bf16[2,256,128]{1,2,0:T(8,128)(2,1)}), bf16[2,2048,128]{1,2,0:T(8,128)(2,1)}) %all-gather.16.cloned.1.call-update) | async-done | bytes 1048592 | tf_op jit(solution)/shard_map/all_gather | solution.py:24
  669.7 5.8 fusion.37
  675.6 20.7 %reduce-scatter.36.cloned.1.call-done = bf16[2,256,128]{1,2,0:T(8,128)(2,1)} async-done(((bf16[2,1024,128]{1,2,0:T(8,128)(2,1)}), bf16[2,256,128]{1,2,0:T(8,128)(2,1)}) %reduce-scatter.36.cloned.1.call-update) | async-done | bytes 131088 | tf_op jit(solution)/shard_map/reduce_scatter | solution.py:18
  696.2 7.2 all_gather.54
  703.6 4.7 fusion.103
  708.3 9.3 fusion.32
  717.6 1.7 copy.77
  719.3 1.2 copy.91
  720.6 64.0 %reduce-scatter.48.cloned.1.call-done = bf16[128,512]{1,0:T(8,128)(2,1)} async-done(((bf16[1024,512]{1,0:T(8,128)(2,1)}), bf16[128,512]{1,0:T(8,128)(2,1)}) %reduce-scatter.48.cloned.1.call-update) | async-done | bytes 131088
  784.6 0.9 reshape.493
  786.4 39.2 %all-gather.18.cloned.1.call-done = bf16[4,1024,128]{1,2,0:T(8,128)(2,1)} async-done(((bf16[4,128,128]{1,2,0:T(8,128)(2,1)}), bf16[4,1024,128]{1,2,0:T(8,128)(2,1)}) %all-gather.18.cloned.1.call-update) | async-done | bytes 1048592 | tf_op jit(solution)/shard_map/all_gather | solution.py:24
  825.6 3.2 fusion.38
  829.2 0.9 copy.93
  830.2 3.4 fusion.13
  833.7 17.1 %reduce-scatter.50.cloned.1.call-done = bf16[128,512]{1,0:T(8,128)(2,1)} async-done(((bf16[512,512]{1,0:T(8,128)(2,1)}), bf16[128,512]{1,0:T(8,128)(2,1)}) %reduce-scatter.50.cloned.1.call-update) | async-done | bytes 131088
  850.8 0.9 reshape.495
  851.8 2.4 fusion.2
  854.1 5.0 fusion.11
  859.2 63.4 %reduce-scatter.38.cloned.1.call-done = bf16[1,512,128]{2,1,0:T(8,128)(2,1)} async-done(((bf16[1,4096,128]{2,1,0:T(8,128)(2,1)}), bf16[1,512,128]{2,1,0:T(8,128)(2,1)}) %reduce-scatter.38.cloned.1.call-update) | async-done | bytes 131088 | tf_op jit(solution)/shard_map/reduce_scatter | solution.py:28
  922.7 21.0 %reduce-scatter.40.cloned.1.call-done = bf16[1,128,128]{2,1,0:T(8,128)(2,1)} async-done(((bf16[1,512,128]{2,1,0:T(8,128)(2,1)}), bf16[1,128,128]{2,1,0:T(8,128)(2,1)}) %reduce-scatter.40.cloned.1.call-update) | async-done | bytes 32784 | tf_op jit(solution)/shard_map/reduce_scatter | solution.py:18
  943.7 1.9 fusion.30
  945.7 22.2 %reduce-scatter.42.cloned.1.call-done = bf16[1,512,128]{2,1,0:T(8,128)(2,1)} async-done(((bf16[1,2048,128]{2,1,0:T(8,128)(2,1)}), bf16[1,512,128]{2,1,0:T(8,128)(2,1)}) %reduce-scatter.42.cloned.1.call-update) | async-done | bytes 131088 | tf_op jit(solution)/shard_map/reduce_scatter | solution.py:18
  967.9 2.2 fusion.31
  970.1 0.8 copy.66
  970.8 21.2 %reduce-scatter.44.cloned.1.call-done = bf16[1,512,128]{1,2,0:T(8,128)(2,1)} async-done(((bf16[1,2048,128]{1,2,0:T(8,128)(2,1)}), bf16[1,512,128]{1,2,0:T(8,128)(2,1)}) %reduce-scatter.44.cloned.1.call-update) | async-done | bytes 131088 | tf_op jit(solution)/shard_map/reduce_scatter | solution.py:18
  992.1 1.7 copy.63
  (91 shorter events, 5.3 us)
Async XLA Ops:
  7.2 9.1 copy-start
  7.2 64.9 %all-gather.20.cloned.1.call-start = ((), (), s32[]{:S(2)}) async-start(), calls=%async_computation.32 | async-start | bytes 1179648 | tf_op jit(solution)/shard_map/all_gather | solution.py:24
  31.5 119.7 %reduce-scatter.46.cloned.1.call-start = ((), (), s32[]{:S(2)}) async-start(), calls=%async_computation.33 | async-start | bytes 1179648
  86.5 114.0 %copy-start.13 = (s32[8]{0:T(128)S(1)}, s32[8]{0:T(128)}, u32[]{:S(2)}) copy-start(s32[8]{0:T(128)} %param.26) | copy-start | bytes 100
  89.4 103.3 %all-gather.10.cloned.1.call-start = ((), (), s32[]{:S(2)}) async-start(), calls=%async_computation.15 | async-start | bytes 1179648 | tf_op jit(solution)/shard_map/all_gather | solution.py:24
  153.0 68.1 %reduce-scatter.22.cloned.1.call-start = ((), (), s32[]{:S(2)}) async-start(), calls=%async_computation.16 | async-start | bytes 655360 | tf_op jit(solution)/shard_map/reduce_scatter | solution.py:18
  200.4 102.2 %copy-start.1 = (bf16[4,1024,128]{1,2,0:T(8,128)(2,1)S(1)}, bf16[4,1024,128]{1,2,0:T(8,128)(2,1)}, u32[]{:S(2)}) copy-start(bf16[4,1024,128]{1,2,0:T(8,128)(2,1)} %all-gather.10.cloned.1.call-done) | copy-start | bytes 3145732
  200.4 101.9 %reduce-scatter.24.cloned.1.call-start = ((), (), s32[]{:S(2)}) async-start(), calls=%async_computation.17 | async-start | bytes 1179648 | tf_op jit(solution)/shard_map/reduce_scatter | solution.py:28
  200.6 114.2 %copy-start.10 = (s32[1,4,8,128]{3,1,2,0:T(4,128)}, s32[1,4,8,128]{3,1,2,0:T(4,128)S(1)}, u32[]{:S(2)}) copy-start(s32[1,4,8,128]{3,1,2,0:T(4,128)S(1)} %copy.84) | copy-start | bytes 49156
  237.9 105.1 %all-gather.12.cloned.1.call-start = ((), (), s32[]{:S(2)}) async-start(), calls=%async_computation.19 | async-start | bytes 1179648 | tf_op jit(solution)/shard_map/all_gather | solution.py:24
  302.3 63.9 %reduce-scatter.26.cloned.1.call-start = ((), (), s32[]{:S(2)}) async-start(), calls=%async_computation.18 | async-start | bytes 655360 | tf_op jit(solution)/shard_map/reduce_scatter | solution.py:18
  314.8 40.9 %copy-start.7 = (bf16[512,128]{1,0:T(8,128)(2,1)S(1)}, bf16[512,128]{1,0:T(8,128)(2,1)}, u32[]{:S(2)}) copy-start(bf16[512,128]{1,0:T(8,128)(2,1)} %param.17) | copy-start | bytes 393220
  314.8 75.6 %reduce-scatter.28.cloned.1.call-start = ((), (), s32[]{:S(2)}) async-start(), calls=%async_computation.20 | async-start | bytes 655360 | tf_op jit(solution)/shard_map/reduce_scatter | solution.py:18
  355.6 121.9 %reduce-scatter.30.cloned.1.call-start = ((), (), s32[]{:S(2)}) async-start(), calls=%async_computation.21 | async-start | bytes 1179648 | tf_op jit(solution)/shard_map/reduce_scatter | solution.py:28
  355.7 57.2 %copy-start.12 = (s32[1,4,8,128]{3,1,2,0:T(4,128)}, s32[1,4,8,128]{3,1,2,0:T(4,128)S(1)}, u32[]{:S(2)}) copy-start(s32[1,4,8,128]{3,1,2,0:T(4,128)S(1)} %copy.85) | copy-start | bytes 49156
  412.9 105.1 %all-gather.14.cloned.1.call-start = ((), (), s32[]{:S(2)}) async-start(), calls=%async_computation.22 | async-start | bytes 1179648 | tf_op jit(solution)/shard_map/all_gather | solution.py:24
  477.5 70.4 %reduce-scatter.32.cloned.1.call-start = ((), (), s32[]{:S(2)}) async-start(), calls=%async_computation.23 | async-start | bytes 655360 | tf_op jit(solution)/shard_map/reduce_scatter | solution.py:18
  527.2 101.3 %reduce-scatter.34.cloned.1.call-start = ((), (), s32[]{:S(2)}) async-start(), calls=%async_computation.24 | async-start | bytes 1179648 | tf_op jit(solution)/shard_map/reduce_scatter | solution.py:28
  554.9 73.6 %copy-start.5 = (bf16[2,256,128]{1,2,0:T(8,128)(2,1)S(1)}, bf16[2,256,128]{1,2,0:T(8,128)(2,1)}, u32[]{:S(2)}) copy-start(bf16[2,256,128]{1,2,0:T(8,128)(2,1)} %reduce-scatter.24.cloned.1.call-done) | copy-start | bytes 393220
  564.1 105.7 %all-gather.16.cloned.1.call-start = ((), (), s32[]{:S(2)}) async-start(), calls=%async_computation.25 | async-start | bytes 1179648 | tf_op jit(solution)/shard_map/all_gather | solution.py:24
  630.1 66.1 %reduce-scatter.36.cloned.1.call-start = ((), (), s32[]{:S(2)}) async-start(), calls=%async_computation.26 | async-start | bytes 655360 | tf_op jit(solution)/shard_map/reduce_scatter | solution.py:18
  675.5 109.1 %reduce-scatter.48.cloned.1.call-start = ((), (), s32[]{:S(2)}) async-start(), calls=%async_computation.34 | async-start | bytes 1179648
  708.3 77.4 %copy-start.3 = (bf16[4,128,128]{1,2,0:T(8,128)(2,1)S(1)}, bf16[4,128,128]{1,2,0:T(8,128)(2,1)}, u32[]{:S(2)}) copy-start(bf16[4,128,128]{1,2,0:T(8,128)(2,1)} %copy.76) | copy-start | bytes 393220
  717.6 112.6 %copy-start.4 = (bf16[1,512,128]{1,2,0:T(8,128)(2,1)S(1)}, bf16[1,512,128]{1,2,0:T(8,128)(2,1)}, u32[]{:S(2)}) copy-start(bf16[1,512,128]{1,2,0:T(8,128)(2,1)} %reduce-scatter.32.cloned.1.call-done) | copy-start | bytes 393220
  720.5 105.1 %all-gather.18.cloned.1.call-start = ((), (), s32[]{:S(2)}) async-start(), calls=%async_computation.27 | async-start | bytes 1179648 | tf_op jit(solution)/shard_map/all_gather | solution.py:24
  786.4 47.1 %copy-start.6 = (bf16[2,256,128]{1,2,0:T(8,128)(2,1)S(1)}, bf16[2,256,128]{1,2,0:T(8,128)(2,1)}, u32[]{:S(2)}) copy-start(bf16[2,256,128]{1,2,0:T(8,128)(2,1)} %reduce-scatter.36.cloned.1.call-done) | copy-start | bytes 393220
  786.4 64.4 %reduce-scatter.50.cloned.1.call-start = ((), (), s32[]{:S(2)}) async-start(), calls=%async_computation.35 | async-start | bytes 655360
  830.1 24.1 %copy-start.11 = (s32[1,4,8,128]{3,1,2,0:T(4,128)S(1)}, s32[1,4,8,128]{3,1,2,0:T(4,128)}, u32[]{:S(2)}) copy-start(s32[1,4,8,128]{3,1,2,0:T(4,128)} %copy-done.10) | copy-start | bytes 49156
  830.1 92.6 %reduce-scatter.38.cloned.1.call-start = ((), (), s32[]{:S(2)}) async-start(), calls=%async_computation.28 | async-start | bytes 1179648 | tf_op jit(solution)/shard_map/reduce_scatter | solution.py:28
  833.5 110.2 %copy-start.2 = (bf16[1,128,2048]{2,1,0:T(8,128)(2,1)S(1)}, bf16[1,128,2048]{2,1,0:T(8,128)(2,1)}, u32[]{:S(2)}) copy-start(bf16[1,128,2048]{2,1,0:T(8,128)(2,1)} %param.22) | copy-start | bytes 1572868
  833.6 111.9 %copy-start.8 = (bf16[2,256,128]{2,1,0:T(8,128)(2,1)}, bf16[2,256,128]{2,1,0:T(8,128)(2,1)S(1)}, u32[]{:S(2)}) copy-start(bf16[2,256,128]{2,1,0:T(8,128)(2,1)S(1)} %copy.61) | copy-start | bytes 393220
  851.8 93.8 %copy-start.9 = (bf16[4,128,128]{2,1,0:T(8,128)(2,1)}, bf16[4,128,128]{2,1,0:T(8,128)(2,1)S(1)}, u32[]{:S(2)}) copy-start(bf16[4,128,128]{2,1,0:T(8,128)(2,1)S(1)} %copy.60) | copy-start | bytes 393220
  859.2 84.5 %reduce-scatter.40.cloned.1.call-start = ((), (), s32[]{:S(2)}) async-start(), calls=%async_computation.29 | async-start | bytes 163840 | tf_op jit(solution)/shard_map/reduce_scatter | solution.py:18
  922.7 45.2 %reduce-scatter.42.cloned.1.call-start = ((), (), s32[]{:S(2)}) async-start(), calls=%async_computation.30 | async-start | bytes 655360 | tf_op jit(solution)/shard_map/reduce_scatter | solution.py:18
  945.6 46.4 %reduce-scatter.44.cloned.1.call-start = ((), (), s32[]{:S(2)}) async-start(), calls=%async_computation.31 | async-start | bytes 655360 | tf_op jit(solution)/shard_map/reduce_scatter | solution.py:18
Sparse Core Ops, SparseCore 0:
  31.7 40.3 all-gather.19
  89.6 61.6 reduce-scatter.45
  154.1 38.5 all-gather.9
  200.5 20.5 reduce-scatter.21
  238.1 64.2 reduce-scatter.23
  304.4 38.5 all-gather.11
  345.7 20.5 reduce-scatter.25
  368.7 21.6 reduce-scatter.27
  413.0 64.4 reduce-scatter.29
  479.4 38.5 all-gather.13
  527.3 20.5 reduce-scatter.31
  564.2 64.2 reduce-scatter.33
  631.1 38.5 all-gather.15
  675.6 20.5 reduce-scatter.35
  720.6 63.8 reduce-scatter.47
  787.0 38.5 all-gather.17
  830.2 20.5 reduce-scatter.49
  859.3 63.3 reduce-scatter.37
  925.1 18.5 reduce-scatter.39
  946.2 21.6 reduce-scatter.41
  970.4 21.6 reduce-scatter.43
where the time goes:
time: 1010 us; the launch traced here: 1000 us
  waiting for transfers between devices  786 us (78%)
  matrix products  122 us (12%)
  blocking collectives  57.3 us (6%)
  local copies, waits for them, and re-layouts  15.4 us (2%)
  between operations  15.1 us (1%)
    reduce_scatter x4, waiting for transfers between devices, leaf_total(): lax.psum_scatter(summands.astype(jnp.bfloat16), 'leaf', scatter_dimension...  257 us
    all_gather x6, waiting for transfers between devices, leaf_gather(): return lax.all_gather(pieces, 'leaf', axis=1, tiled=True)  225 us
    reduce_scatter x8, waiting for transfers between devices, row_total(): lax.psum_scatter(summands.astype(jnp.bfloat16), 'row', scatter_dimension=...  161 us
    unnamed x24, waiting for transfers between devices  143 us
    all_gather x8, blocking collectives, row_gather(): return lax.all_gather(pieces, 'row', axis=1, tiled=True)  57.3 us
    dot_general x3, matrix products, level_forward(): jnp.einsum('smn,snp->smp', inverse, columns, preferred_element_type=jnp.f...  24.3 us
  transfers between devices with their start and end apart: 21, of which 21 were waited for; matrix products, arithmetic and copies ran while one was open for 3% of the time, Pallas kernels for 0%

commit v1 on v0

v1 whole, which is shorter than its diff:
```python
import functools

import jax
import jax.numpy as jnp
from jax import lax
from jax.experimental import pallas as pl
from jax.experimental.pallas import tpu as pltpu
from jax.sharding import PartitionSpec as P

LOWER_ORDER = 4096
MIDDLE_ORDER = 8192
ROOT_ORDER = 16384
BLOCK = 128
PANEL = 512
LEVELS = 4


def exchange_kernel(axis, n, reduce, gather, has_base, *refs):
    refs = list(refs)
    parts_ref = refs.pop(0)
    base_ref = refs.pop(0) if has_base else None
    out_ref = refs.pop(0)
    near_land, staged, far_land, whole, sems = refs
    far_count = n // 2
    me = lax.axis_index(axis)
    near = lax.rem(me, 2)
    far = me // 2
    partner = far * 2 + (1 - near)

    def far_at(k):
        return lax.rem(far + k, far_count)

    def device(index):
        return {axis: index}

    def remote(src, dst, kind, k, target):
        return pltpu.make_async_remote_copy(
            src_ref=src,
            dst_ref=dst,
            send_sem=sems.at[0, kind, k],
            recv_sem=sems.at[1, kind, k],
            device_id=device(target),
            device_id_type=pl.DeviceIdType.MESH,
        )

    barrier = pltpu.get_barrier_semaphore()
    pl.semaphore_signal(
        barrier, inc=1, device_id=device(partner), device_id_type=pl.DeviceIdType.MESH
    )
    for k in range(1, far_count):
        pl.semaphore_signal(
            barrier,
            inc=1,
            device_id=device(far_at(k) * 2 + near),
            device_id_type=pl.DeviceIdType.MESH,
        )
    pl.semaphore_wait(barrier, far_count)

    order = list(range(1, far_count)) + [0]
    sends = []
    if reduce:
        to_partner = {}
        for k in order:
            to_partner[k] = remote(
                parts_ref.at[:, far_at(k) * 2 + (1 - near)], near_land.at[k], 0, k, partner
            )
            to_partner[k].start()
        to_far = {}
        total = None
        for k in order:
            to_partner[k].wait_recv()
            pair = parts_ref[:, far_at(k) * 2 + near].astype(jnp.float32) + near_land[k].astype(
                jnp.float32
            )
            if k == 0:
                total = pair
            else:
                staged[k] = pair.astype(staged.dtype)
                to_far[k] = remote(
                    staged.at[k], far_land.at[k], 1, k, far_at(k) * 2 + near
                )
                to_far[k].start()
        for k in range(1, far_count):
            to_far[k].wait_recv()
            total = total + far_land[k].astype(jnp.float32)
        if has_base:
            total = base_ref[...] - total
        mine = total.astype(out_ref.dtype)
        sends += [to_partner[k] for k in order] + [to_far[k] for k in range(1, far_count)]
    else:
        mine = parts_ref[...]
    if gather:
        whole[:, me] = mine
        along = {}
        for k in range(1, far_count):
            along[k] = remote(whole.at[:, me], whole.at[:, me], 2, k, far_at(k) * 2 + near)
            along[k].start()
        passed = {0: remote(whole.at[:, me], whole.at[:, me], 3, 0, partner)}
        passed[0].start()
        for k in range(1, far_count):
            along[k].wait_recv()
            came = lax.rem(far + far_count - k, far_count) * 2 + near
            passed[k] = remote(whole.at[:, came], whole.at[:, came], 3, k, partner)
            passed[k].start()
        for k in range(far_count):
            passed[k].wait_recv()
        sends += [along[k] for k in range(1, far_count)] + [passed[k] for k in range(far_count)]
    for copy in sends:
        copy.wait_send()
    out_ref[...] = whole[...] if gather else mine


class Exchanges:
    def __init__(self):
        self.calls = 0

    def run(self, parts, axis, reduce, gather, base=None):
        n = lax.axis_size(axis)
        if reduce:
            s, rows, p = parts.shape
            w = rows // n
            operands = [parts.astype(jnp.bfloat16).reshape(s, n, w, p)]
        else:
            s, w, p = parts.shape
            operands = [parts]
        if base is not None:
            operands.append(base)
        far_count = n // 2
        slots = (far_count if reduce else 1, s if reduce else 1, w if reduce else 16, p)
        out_shape = (s, n, w, p) if gather else (s, w, p)
        whole_shape = (s, n, w, p) if gather else (1, 1, 16, p)
        call_id = self.calls
        self.calls += 1
        out = pl.pallas_call(
            functools.partial(exchange_kernel, axis, n, reduce, gather, base is not None),
            out_shape=jax.ShapeDtypeStruct(out_shape, jnp.bfloat16),
            in_specs=[pl.BlockSpec(memory_space=pltpu.VMEM)] * len(operands),
            out_specs=pl.BlockSpec(memory_space=pltpu.VMEM),
            scratch_shapes=[
                pltpu.VMEM(slots, jnp.bfloat16),
                pltpu.VMEM(slots, jnp.bfloat16),
                pltpu.VMEM(slots, jnp.bfloat16),
                pltpu.VMEM(whole_shape, jnp.bfloat16),
                pltpu.SemaphoreType.DMA((2, 4, far_count)),
            ],
            compiler_params=pltpu.CompilerParams(
                collective_id=call_id, has_side_effects=True, vmem_limit_bytes=16 << 20
            ),
            name=f"exchange_{axis}_{call_id}",
        )(*operands)
        return out.reshape(s, n * w, p) if gather else out

    def gather(self, pieces, axis):
        return self.run(pieces, axis, False, True)

    def total(self, summands, axis, base=None):
        return self.run(summands, axis, True, False, base)

    def everywhere(self, summands, axis, base=None):
        return self.run(summands, axis, True, True, base)


def product(spec, left, right):
    return jnp.einsum(spec, left, right, preferred_element_type=jnp.float32)


def target_places(leaf_parent, leaf_blocks, block_index):
    offset = jnp.arange(BLOCK, dtype=jnp.int32)[None, :]
    owners = leaf_parent if block_index < 2 else leaf_parent // 2
    if block_index == 3:
        owners = jnp.zeros_like(leaf_parent)
    owners = owners[:, None] + 0 * offset
    return owners, leaf_blocks[:, block_index : block_index + 1] * BLOCK + offset


def picker(leaf_parent, leaf_blocks, block_indices, row_devices, separators, start, window):
    slots = []
    for block_index in block_indices:
        owners, places = target_places(leaf_parent, leaf_blocks, block_index)
        inside = (places >= start) & (places < start + window)
        slot = jnp.where(inside, owners * window + places - start, -1)
        leaves = slot.shape[0]
        pieces = row_devices // LEVELS
        slots.append(slot.reshape(leaves, pieces, BLOCK // pieces).transpose(1, 0, 2).reshape(-1))
    slot = jnp.concatenate(slots)
    slot_ids = jnp.arange(separators * window, dtype=jnp.int32)
    return (slot_ids[:, None] == slot[None, :]).astype(jnp.bfloat16)


def body(
    leaf_probes,
    lower_probes,
    middle_probes,
    root_probes,
    leaf_inverse,
    lower_inverse,
    middle_inverse,
    root_inverse,
    leaf_panel,
    lower_to_middle,
    lower_to_root,
    middle_to_root,
    leaf_parent,
    leaf_blocks,
):
    f32, bf16 = jnp.float32, jnp.bfloat16
    links = Exchanges()
    leaf_devices = lax.axis_size("leaf")
    row_devices = lax.axis_size("row")
    position = lax.axis_index("leaf") * row_devices + lax.axis_index("row")
    devices = leaf_devices * row_devices
    probe_count = leaf_probes.shape[-1]
    counts = (4, 2, 1)
    windows = [order // devices for order in (LOWER_ORDER, MIDDLE_ORDER, ROOT_ORDER)]
    blocks_of = ((0, 1), (2,), (3,))
    pickers = [
        picker(
            leaf_parent,
            leaf_blocks,
            blocks_of[m],
            row_devices,
            counts[m],
            position * windows[m],
            windows[m],
        )
        for m in range(3)
    ]
    per_block = leaf_devices * BLOCK
    spans = ((0, 2 * per_block), (2 * per_block, 3 * per_block), (3 * per_block, 4 * per_block))

    leaf_columns = links.gather(leaf_probes, "row")
    leaf_solved = product("lab,lbp->lap", leaf_inverse, leaf_columns).astype(bf16)
    leaf_whole = links.gather(leaf_solved, "row")
    leaf_update = product("lkb,lbp->lkp", leaf_panel, leaf_whole).astype(bf16)
    received = links.gather(links.gather(leaf_update, "leaf"), "row")[0]
    added = [
        jnp.dot(
            pickers[m], received[spans[m][0] : spans[m][1]], preferred_element_type=f32
        ).reshape(counts[m], windows[m], probe_count)
        for m in range(3)
    ]
    lower_input = (lower_probes.astype(f32) - added[0]).astype(bf16)
    middle_base = middle_probes.astype(f32) - added[1]
    root_base = root_probes[None].astype(f32) - added[2]

    def own(block, axis):
        piece = block.shape[1] // lax.axis_size(axis)
        return lax.dynamic_slice_in_dim(block, lax.axis_index(axis) * piece, piece, axis=1)

    lower_columns = links.gather(lower_input, "row")
    lower_block = links.everywhere(product("smn,snp->smp", lower_inverse, lower_columns), "leaf")
    lower_solved = own(lower_block, "leaf").astype(f32)
    to_middle = product("san,snp->sap", lower_to_middle, lower_block)
    to_middle = to_middle.reshape(2, 2, to_middle.shape[1], probe_count).sum(axis=1)
    middle_in = links.everywhere(to_middle, "row", middle_base)
    to_root = product("san,snp->sap", lower_to_root, lower_block).sum(axis=0, keepdims=True)
    middle_block = links.everywhere(product("smn,snp->smp", middle_inverse, middle_in), "leaf")
    middle_solved = own(middle_block, "leaf").astype(f32)
    to_root = to_root + product("san,snp->sap", middle_to_root, middle_block).sum(
        axis=0, keepdims=True
    )
    root_in = links.everywhere(to_root, "row", root_base)
    root_block = links.everywhere(product("smn,snp->smp", root_inverse[None], root_in), "leaf")

    root_columns = links.everywhere(product("smn,smp->snp", root_inverse[None], root_block), "row")
    root_solution = own(root_columns, "row")
    middle_reduced = links.everywhere(
        product("san,ap->snp", middle_to_root, root_columns[0]), "leaf", middle_solved
    )
    middle_columns = links.everywhere(product("smn,smp->snp", middle_inverse, middle_reduced), "row")
    middle_solution = own(middle_columns, "row")
    lower_drop = product("san,ap->snp", lower_to_root, root_columns[0])
    lower_drop = lower_drop + product(
        "san,sap->snp", lower_to_middle, jnp.repeat(middle_columns, 2, axis=0)
    )
    lower_reduced = links.everywhere(lower_drop, "leaf", lower_solved)
    lower_solution = links.total(product("smn,smp->snp", lower_inverse, lower_reduced), "row")

    sources = (lower_solution, middle_solution, root_solution)
    values = jnp.concatenate(
        [
            product("sm,sp->mp", pickers[m], sources[m].reshape(-1, probe_count)).astype(bf16)
            for m in range(3)
        ]
    )
    ancestor = links.total(links.total(values[None], "row"), "leaf")
    leaf_reduced = links.total(
        product("lkb,lkp->lbp", leaf_panel, ancestor), "row", leaf_solved.astype(f32)
    )
    leaf_solution = links.total(product("lab,lap->lbp", leaf_inverse, leaf_reduced), "row")
    return (leaf_solution, lower_solution, middle_solution, root_solution[0])


def solution(mesh):
    placed = (
        P("leaf", "row", None),
        P(None, ("leaf", "row"), None),
        P(None, ("leaf", "row"), None),
        P(("leaf", "row"), None),
        P("leaf", "row", None),
        P(None, "row", "leaf"),
        P(None, "row", "leaf"),
        P("row", "leaf"),
        P("leaf", "row", None),
        P(None, "leaf", "row"),
        P(None, "leaf", "row"),
        P(None, "leaf", "row"),
        P(),
        P(),
    )
    return jax.shard_map(
        body,
        mesh=mesh,
        in_specs=placed,
        out_specs=(
            P("leaf", "row", None),
            P(None, ("leaf", "row"), None),
            P(None, ("leaf", "row"), None),
            P(("leaf", "row"), None),
        ),
        check_vma=False,
    )
```

time: 1010 us -> 477 us (0.47)
  waiting for transfers between devices: 786 us -> 0 us
  Pallas kernels: 0 us -> 335 us
  blocking collectives: 57.3 us -> 0 us
  matrix products: 122 us -> 98.7 us
  local copies, waits for them, and re-layouts: 15.4 us -> 29.9 us
  between operations: 15.1 us -> 1.68 us
    reduce_scatter x12 -> x0, waiting for transfers between devices: 417 us -> none  [the longest x4 257 us: leaf_total(): lax.psum_scatter(summands.astype(jnp.bfloat16), 'leaf', scatter_dimension...]
    pallas_call x0 -> x19, Pallas kernels: none -> 335 us  [run(): pl.pallas_call(functools.partial(exchange_kernel, axis, n, reduce, gather...]
    all_gather x6 -> x0, waiting for transfers between devices: 225 us -> none  [leaf_gather(): return lax.all_gather(pieces, 'leaf', axis=1, tiled=True)]
    unnamed x24 -> x0, waiting for transfers between devices: 143 us -> none
    all_gather x8 -> x0, blocking collectives: 57.3 us -> none  [row_gather(): return lax.all_gather(pieces, 'row', axis=1, tiled=True)]
    dot_general x22, matrix products: 122 us -> 98.7 us  [the longest x19 95.5 us: product(): return jnp.einsum(spec, left, right, preferred_element_type=jnp.float32)]
    convert_element_type x0 -> x12, local copies, waits for them, and re-layouts: none -> 15.2 us  [run(): operands = [parts.astype(jnp.bfloat16).reshape(s, n, w, p)]]
  transfers between devices with their start and end apart: 21 -> 0, of which waited for: 21 -> 0; matrix products, arithmetic and copies ran while one was open for 3% -> 0% of each run, Pallas kernels for 0% -> 0%
where the time goes in v1:
time: 477 us; the launch traced here: 469 us
  Pallas kernels  335 us (70%)
  matrix products  98.7 us (21%)
  local copies, waits for them, and re-layouts  29.9 us (6%)
    pallas_call x19, Pallas kernels, run(): pl.pallas_call(functools.partial(exchange_kernel, axis, n, reduce, gather...  335 us
    dot_general x19, matrix products, product(): return jnp.einsum(spec, left, right, preferred_element_type=jnp.float32)  95.5 us
    convert_element_type x12, local copies, waits for them, and re-layouts, run(): operands = [parts.astype(jnp.bfloat16).reshape(s, n, w, p)]  15.2 us
    unnamed x46, local copies, waits for them, and re-layouts  12.5 us

profile of v1, /device:TPU:0, one launch (start us, length us, event | category | flops | bytes accessed | tf_op | source)
XLA Modules:
  0.0 469.5 jit_solution(10852431093304883386)
XLA Ops:
  0.7 0.8 fusion.73
  1.5 0.8 multiply_bitcast_fusion
  2.5 0.9 copy-done.11
  3.4 8.3 %exchange_row_0.1 = bf16[1,4,512,128]{3,2,1,0:T(8,128)(2,1)S(1)} custom-call(bf16[1,512,128]{2,1,0:T(8,128)(2,1)S(1)} %copy-done.11), custom_call_target="tpu_custom_call" | custom-call | tf_op jit(solution)/shard_map/exchange_row_0/pallas_call | solution.py:134
  11.7 0.7 fusion.74
  12.5 7.0 %exchange_row_1.1 = bf16[1,4,512,128]{3,2,1,0:T(8,128)(2,1)S(1)} custom-call(bf16[1,512,128]{2,1,0:T(8,128)(2,1)S(1)} %get-tuple-element.13.refs_0_), custom_call_target="tpu_custom_call" | custom-call | tf_op jit(solution)/shard_map/exchange_row_1/pallas_call | solution.py:134
  19.8 11.5 %exchange_leaf_2.1 = bf16[1,8,128,128]{3,2,1,0:T(8,128)(2,1)S(1)} custom-call(bf16[1,128,128]{2,1,0:T(8,128)(2,1)S(1)} %fusion.47.refs_0_), custom_call_target="tpu_custom_call" | custom-call | tf_op jit(solution)/shard_map/exchange_leaf_2/pallas_call | solution.py:134
  31.3 9.5 %exchange_row_3.1 = bf16[1,4,1024,128]{3,2,1,0:T(8,128)(2,1)S(1)} custom-call(bf16[1,1024,128]{2,1,0:T(8,128)(2,1)S(1)} %bitcast.194), custom_call_target="tpu_custom_call" | custom-call | tf_op jit(solution)/shard_map/exchange_row_3/pallas_call | solution.py:134
  40.8 1.2 fusion.30.refs_1_
  42.0 1.2 fusion.34.refs_1_
  43.2 0.8 fusion.41.refs_0_
  44.0 7.0 %exchange_row_4.1 = bf16[4,4,128,128]{3,2,1,0:T(8,128)(2,1)S(1)} custom-call(bf16[4,128,128]{2,1,0:T(8,128)(2,1)S(1)} %fusion.41.refs_0_), custom_call_target="tpu_custom_call" | custom-call | tf_op jit(solution)/shard_map/exchange_row_4/pallas_call | solution.py:134
  51.0 1.5 fusion.25
  52.5 1.3 copy.42
  53.9 1.2 copy-done.3
  55.1 36.9 %exchange_leaf_5.1 = bf16[4,8,128,128]{3,2,1,0:T(8,128)(2,1)S(1)} custom-call(bf16[4,8,128,128]{3,2,1,0:T(8,128)(2,1)S(1)} %bitcast.177), custom_call_target="tpu_custom_call" | custom-call | tf_op jit(solution)/shard_map/exchange_leaf_5/pallas_call | solution.py:134
  92.0 0.7 dynamic-slice_convert_fusion.refs_1_
  92.8 7.2 %bitcast_reduce_fusion = bf16[2,1024,128]{1,2,0:T(8,128)(2,1)} fusion(bf16[4,1024,128]{2,1,0:T(8,128)(2,1)S(1)} %bitcast.165, bf16[4,1024,1024]{2,1,0:T(8,128)(2,1)} %param.23), kind=kOutput, calls=%fused_computation.22 | convolution fusion | flops 1074003968 | bytes 9961472 | tf_op jit(solution)/shard_map/san,snp->sap/dot_general | solution.py:164
  100.0 2.0 copy.45
  102.0 1.0 copy-done.5
  103.1 0.9 copy-done.10
  104.0 12.4 %exchange_row_6.1 = bf16[2,4,256,128]{3,2,1,0:T(8,128)(2,1)S(1)} custom-call(bf16[2,4,256,128]{3,2,1,0:T(8,128)(2,1)S(1)} %bitcast.189, f32[2,256,128]{2,1,0:T(8,128)S(1)} %copy-done.10), custom_call_target="tpu_custom_call" | custom-call | tf_op jit(solution)/shard_map/exchange_row_6/pallas_call | solution.py:134
  116.5 7.3 %fusion.4 = bf16[2,2048,128]{1,2,0:T(8,128)(2,1)} fusion(bf16[2,1024,128]{2,1,0:T(8,128)(2,1)S(1)} %bitcast.182, bf16[2,2048,1024]{2,1,0:T(8,128)(2,1)} %param.20), kind=kOutput, calls=%fused_computation.8 | convolution fusion | flops 1074266112 | bytes 9961472 | tf_op jit(solution)/shard_map/smn,snp->smp/dot_general | solution.py:164
  123.8 2.4 copy.47
  126.2 1.2 copy-done.4
  127.4 40.0 %exchange_leaf_7.1 = bf16[2,8,256,128]{3,2,1,0:T(8,128)(2,1)S(1)} custom-call(bf16[2,8,256,128]{3,2,1,0:T(8,128)(2,1)S(1)} %bitcast.178), custom_call_target="tpu_custom_call" | custom-call | tf_op jit(solution)/shard_map/exchange_leaf_7/pallas_call | solution.py:134
  167.4 1.0 copy-done.1
  168.4 0.7 dynamic-slice_convert_fusion.1.refs_1_
  169.2 12.8 %convolution_bitcast_fusion = f32[128,2048]{1,0:T(8,128)} fusion(bf16[2,2048,128]{2,1,0:T(8,128)(2,1)} %bitcast.173, bf16[2,2048,2048]{2,1,0:T(8,128)(2,1)} %param.25), kind=kOutput, calls=%fused_computation.10 | convolution fusion | flops 2147483648 | bytes 18874368 | tf_op jit(solution)/shard_map/san,snp->sap/dot_general | solution.py:164
  182.0 12.5 %fusion.12 = bf16[2048,128]{0,1:T(8,128)(2,1)} fusion(f32[128,2048]{1,0:T(8,128)} %convolution_bitcast_fusion, bf16[4,1024,128]{2,1,0:T(8,128)(2,1)S(1)} %bitcast.166, bf16[4,2048,1024]{2,1,0:T(8,128)(2,1)} %param.24), kind=kOutput, calls=%fused_computation.21 | convolution fusion | flops 2148007936 | bytes 19398656 | tf_op jit(solution)/shard_map/san,snp->sap/dot_general | solution.py:164
  194.4 1.3 copy.49
  195.8 0.9 copy-done.9
  196.7 12.5 %exchange_row_8.1 = bf16[1,4,512,128]{3,2,1,0:T(8,128)(2,1)S(1)} custom-call(bf16[1,4,512,128]{3,2,1,0:T(8,128)(2,1)S(1)} %bitcast.190, f32[1,512,128]{2,1,0:T(8,128)S(1)} %copy-done.9), custom_call_target="tpu_custom_call" | custom-call | tf_op jit(solution)/shard_map/exchange_row_8/pallas_call | solution.py:134
  209.2 12.7 %fusion = bf16[4096,128]{0,1:T(8,128)(2,1)} fusion(bf16[2048,128]{1,0:T(8,128)(2,1)S(1)} %bitcast.183, bf16[4096,2048]{1,0:T(8,128)(2,1)} %param.21), kind=kOutput, calls=%fused_computation.1 | convolution fusion | flops 2148007936 | bytes 18350080 | tf_op jit(solution)/shard_map/smn,snp->smp/dot_general | solution.py:164
  221.9 1.6 copy.50
  223.5 40.2 %exchange_leaf_9.1 = bf16[1,8,512,128]{3,2,1,0:T(8,128)(2,1)S(1)} custom-call(bf16[1,8,512,128]{3,2,1,0:T(8,128)(2,1)S(1)} %bitcast.179), custom_call_target="tpu_custom_call" | custom-call | tf_op jit(solution)/shard_map/exchange_leaf_9/pallas_call | solution.py:134
  263.7 8.2 %fusion.9 = bf16[2048,128]{0,1:T(8,128)(2,1)S(1)} fusion(bf16[4096,128]{1,0:T(8,128)(2,1)S(1)} %bitcast.171, bf16[4096,2048]{1,0:T(8,128)(2,1)} %param.21), kind=kOutput, calls=%fused_computation.18 | convolution fusion | flops 2147745792 | bytes 18350080 | tf_op jit(solution)/shard_map/smn,smp->snp/dot_general | solution.py:164
  272.1 12.6 %exchange_row_10.1 = bf16[1,4,512,128]{3,2,1,0:T(8,128)(2,1)S(1)} custom-call(bf16[1,4,512,128]{3,2,1,0:T(8,128)(2,1)S(1)} %bitcast.191), custom_call_target="tpu_custom_call" | custom-call | tf_op jit(solution)/shard_map/exchange_row_10/pallas_call | solution.py:134
  285.4 1.4 fusion.29
  286.8 9.1 %fusion.5 = bf16[2,2048,128]{1,2,0:T(8,128)(2,1)} fusion(bf16[2048,128,1]{1,0,2:T(8,128)(2,1)S(1)} %bitcast.169, bf16[2,2048,2048]{2,1,0:T(8,128)(2,1)} %param.25), kind=kOutput, calls=%fused_computation.9 | convolution fusion | flops 2148007936 | bytes 18350080 | tf_op jit(solution)/shard_map/san,ap->snp/dot_general | solution.py:164
  296.0 2.5 copy.54
  298.5 1.2 copy-done.2
  299.7 40.1 %exchange_leaf_11.1 = bf16[2,8,256,128]{3,2,1,0:T(8,128)(2,1)S(1)} custom-call(bf16[2,8,256,128]{3,2,1,0:T(8,128)(2,1)S(1)} %bitcast.175, f32[2,256,128]{2,1,0:T(8,128)S(1)} %copy-done.8), custom_call_target="tpu_custom_call" | custom-call | tf_op jit(solution)/shard_map/exchange_leaf_11/pallas_call | solution.py:134
  339.8 4.7 %fusion.26 = bf16[2,1024,128]{1,2,0:T(8,128)(2,1)S(1)} fusion(bf16[2,2048,128]{2,1,0:T(8,128)(2,1)S(1)} %bitcast.163, bf16[2,2048,1024]{2,1,0:T(8,128)(2,1)} %param.20), kind=kOutput, calls=%fused_computation.42 | convolution fusion | flops 1074003968 | bytes 9961472 | tf_op jit(solution)/shard_map/smn,smp->snp/dot_general | solution.py:164
  344.6 1.0 copy.56
  345.6 1.0 copy-done.6
  346.6 12.5 %exchange_row_12.1 = bf16[2,4,256,128]{3,2,1,0:T(8,128)(2,1)S(1)} custom-call(bf16[2,4,256,128]{3,2,1,0:T(8,128)(2,1)S(1)} %bitcast.192), custom_call_target="tpu_custom_call" | custom-call | tf_op jit(solution)/shard_map/exchange_row_12/pallas_call | solution.py:134
  359.2 1.0 copy.57
  360.2 1.4 fusion.28
  361.6 1.2 broadcast_in_dim.10
  362.8 8.3 %fusion.75 = f32[128,4,1024]{2,0,1:T(8,128)S(1)} fusion(bf16[2048,128,1]{1,0,2:T(8,128)(2,1)S(1)} %bitcast.170, bf16[4,2048,1024]{2,1,0:T(8,128)(2,1)} %param.24), kind=kOutput, calls=%fused_computation.107 | convolution fusion | flops 2147483648 | bytes 19398656 | tf_op jit(solution)/shard_map/san,ap->snp/dot_general | solution.py:164
  371.1 2.3 fusion.13
  373.4 1.9 copy.58
  375.3 0.9 copy-done.7
  376.3 40.1 %exchange_leaf_13.1 = bf16[4,8,128,128]{3,2,1,0:T(8,128)(2,1)S(1)} custom-call(bf16[4,8,128,128]{3,2,1,0:T(8,128)(2,1)S(1)} %bitcast.176, f32[4,128,128]{2,1,0:T(8,128)S(1)} %copy-done.7), custom_call_target="tpu_custom_call" | custom-call | tf_op jit(solution)/shard_map/exchange_leaf_13/pallas_call | solution.py:134
  416.4 3.0 fusion.27
  419.7 6.2 %exchange_row_14.1 = bf16[4,128,128]{2,1,0:T(8,128)(2,1)S(1)} custom-call(bf16[4,4,128,128]{3,2,1,0:T(8,128)(2,1)S(1)} %bitcast.186), custom_call_target="tpu_custom_call" | custom-call | tf_op jit(solution)/shard_map/exchange_row_14/pallas_call | solution.py:134
  426.0 1.3 fusion.8
  427.2 1.1 pad_maximum_fusion
  428.3 10.4 %exchange_row_15.1 = bf16[1,1024,128]{2,1,0:T(8,128)(2,1)S(1)} custom-call(bf16[1,4,1024,128]{3,2,1,0:T(8,128)(2,1)S(1)} %bitcast.174), custom_call_target="tpu_custom_call" | custom-call | tf_op jit(solution)/shard_map/exchange_row_15/pallas_call | solution.py:134
  438.7 13.3 %exchange_leaf_16.1 = bf16[1,128,128]{2,1,0:T(8,128)(2,1)S(1)} custom-call(bf16[1,8,128,128]{3,2,1,0:T(8,128)(2,1)S(1)} %bitcast.195), custom_call_target="tpu_custom_call" | custom-call | tf_op jit(solution)/shard_map/exchange_leaf_16/pallas_call | solution.py:134
  452.7 7.3 %exchange_row_17.1 = bf16[1,512,128]{2,1,0:T(8,128)(2,1)S(1)} custom-call(bf16[1,4,512,128]{3,2,1,0:T(8,128)(2,1)S(1)} %bitcast.184, f32[1,512,128]{2,1,0:T(8,128)S(1)} %get-tuple-element.12.refs_1_), custom_call_target="tpu_custom_call" | custom-call | tf_op jit(solution)/shard_map/exchange_row_17/pallas_call | solution.py:134
  460.7 6.9 %exchange_row_18.1 = bf16[1,512,128]{2,1,0:T(8,128)(2,1)S(1)} custom-call(bf16[1,4,512,128]{3,2,1,0:T(8,128)(2,1)S(1)} %bitcast.187), custom_call_target="tpu_custom_call" | custom-call | tf_op jit(solution)/shard_map/exchange_row_18/pallas_call | solution.py:134
  467.6 0.7 copy.77
  (51 shorter events, 3.8 us)
Async XLA Ops:
  0.6 11.1 %copy-start = (bf16[1,512,2048]{2,1,0:T(8,128)(2,1)S(1)}, bf16[1,512,2048]{2,1,0:T(8,128)(2,1)}, u32[]{:S(2)}) copy-start(bf16[1,512,2048]{2,1,0:T(8,128)(2,1)} %param.18) | copy-start | bytes 6291460
  2.5 0.9 copy-start.11
  3.4 16.1 %copy-start.13 = (bf16[1,128,2048]{2,1,0:T(8,128)(2,1)S(1)}, bf16[1,128,2048]{2,1,0:T(8,128)(2,1)}, u32[]{:S(2)}) copy-start(bf16[1,128,2048]{2,1,0:T(8,128)(2,1)} %param.22) | copy-start | bytes 1572868
  3.4 37.4 %copy-start.17 = (bf16[2,256,128]{2,1,0:T(8,128)(2,1)S(1)}, bf16[2,256,128]{2,1,0:T(8,128)(2,1)}, u32[]{:S(2)}) copy-start(bf16[2,256,128]{2,1,0:T(8,128)(2,1)} %param.16) | copy-start | bytes 393220
  3.4 38.6 %copy-start.18 = (bf16[512,128]{1,0:T(8,128)(2,1)S(1)}, bf16[512,128]{1,0:T(8,128)(2,1)}, u32[]{:S(2)}) copy-start(bf16[512,128]{1,0:T(8,128)(2,1)} %param.17) | copy-start | bytes 393220
  12.4 30.8 %copy-start.19 = (bf16[4,128,128]{2,1,0:T(8,128)(2,1)S(1)}, bf16[4,128,128]{2,1,0:T(8,128)(2,1)}, u32[]{:S(2)}) copy-start(bf16[4,128,128]{2,1,0:T(8,128)(2,1)} %param.15) | copy-start | bytes 393220
  19.8 31.3 %copy-start.12 = (bf16[4,1024,512]{2,1,0:T(8,128)(2,1)S(1)}, bf16[4,1024,512]{2,1,0:T(8,128)(2,1)}, u32[]{:S(2)}) copy-start(bf16[4,1024,512]{2,1,0:T(8,128)(2,1)} %param.19) | copy-start | bytes 12582916
  53.9 1.2 copy-start.3
  102.0 1.0 copy-start.5
  103.1 0.9 copy-start.10
  126.2 1.2 copy-start.4
  167.4 1.0 copy-start.1
  195.8 1.0 copy-start.9
  284.7 0.7 copy-start.15
  286.8 11.6 %copy-start.8 = (f32[2,256,128]{2,1,0:T(8,128)S(1)}, f32[2,256,128]{2,1,0:T(8,128)}, u32[]{:S(2)}) copy-start(f32[2,256,128]{2,1,0:T(8,128)} %dynamic-slice_convert_fusion.1.refs_1_) | copy-start | bytes 786436
  298.5 1.2 copy-start.2
  345.6 1.0 copy-start.6
  359.1 11.9 %copy-start.16 = (bf16[2,256,128]{2,1,0:T(8,128)(2,1)}, bf16[2,256,128]{2,1,0:T(8,128)(2,1)S(1)}, u32[]{:S(2)}) copy-start(bf16[2,256,128]{2,1,0:T(8,128)(2,1)S(1)} %constant_dynamic-slice_fusion) | copy-start | bytes 393220
  360.2 10.9 %slice-start = ((s8[8388608]{0:T(1024)(128)(4,1)}), s8[4194304]{0:T(1024)(128)(4,1)S(1)}, s32[]{:S(2)}) async-start(s8[8388608]{0:T(1024)(128)(4,1)} %bitcast.197), calls=%async_computation | async-start | bytes 8388608
  362.8 8.3 %slice-start.1 = ((s8[8388608]{0:T(1024)(128)(4,1)}), s8[4194304]{0:T(1024)(128)(4,1)S(1)}, s32[]{:S(2)}) async-start(s8[8388608]{0:T(1024)(128)(4,1)} %bitcast.197), calls=%async_computation.1 | async-start | bytes 8388608
  375.3 1.0 copy-start.7
  419.7 32.3 %copy-start.14 = (bf16[1,128,2048]{2,1,0:T(8,128)(2,1)S(1)}, bf16[1,128,2048]{2,1,0:T(8,128)(2,1)}, u32[]{:S(2)}) copy-start(bf16[1,128,2048]{2,1,0:T(8,128)(2,1)} %param.22) | copy-start | bytes 1572868
